TPU v7x, 256 devices: a whole 4x4x8 slice. The times are simulated.
256 devices in a mesh: outer: 8 (over x, core), inner: 32 (over z, y).
Axes of the slice: x: 4, y: 4, z: 8, core: 2. Of those that a mesh axis runs over, the one named last changes fastest.
Arguments:
- query: bfloat16 [32768, 512], P(('outer', 'inner')), may hold values from -250 to 250
- key: bfloat16 [32768, 128], P(('outer', 'inner')), may hold values from -6 to 6
- value: bfloat16 [32768, 128], P(('outer', 'inner')), may hold values from -6 to 6
- grad_out: bfloat16 [32768, 512], P(('outer', 'inner')), may hold values from -6 to 6
- stretch_order: int32 [64], replicated, may hold values from 0 to 63, each once
Outputs:
- grad_query: bfloat16 [32768, 512], P(('outer', 'inner'))
- grad_key: bfloat16 [32768, 128], P(('outer', 'inner'))
- grad_value: bfloat16 [32768, 128], P(('outer', 'inner'))
Inputs may be any that keep to these rules, and one draw needn't show every extreme that they name: `stretch_order`: a permutation of the 64 blocks; the same for every group.
All inputs are finite; a program needn't handle non-finite values.
Results may differ from a plain program's by a relative error of at most 0.014.
The roundings to bfloat16 on the way count: a program that leaves them out, or rounds other values in their place, can miss the bound.
Values may be sent and summed in bfloat16 or wider, within the bound.
A program may use at most 128 MiB of HBM per device.

v0:
```python
import jax
import jax.numpy as jnp
from jax import lax
from jax.sharding import PartitionSpec as P


def shifted(value, axis, steps):
    count = lax.axis_size(axis)
    first, last = (max(0, -steps), min(count, count - steps))
    return lax.ppermute(value, axis, [(source, source + steps) for source in range(first, last)])


def attend_block(queries, grads, keys, values, allowed):
    dh = keys.shape[1]
    heads = queries.shape[1] // dh
    scale = float(dh) ** (-0.5)
    grad_keys = jnp.zeros(keys.shape, jnp.float32)
    grad_values = jnp.zeros(values.shape, jnp.float32)
    pieces = []
    for head in range(heads):
        q_head = queries[:, head * dh : (head + 1) * dh]
        g_head = grads[:, head * dh : (head + 1) * dh]
        scores = jnp.where(
            allowed, jnp.dot(q_head, keys.T, preferred_element_type=jnp.float32) * scale, -jnp.inf
        )
        top = jnp.max(scores, axis=1, keepdims=True)
        expo = jnp.exp(scores - top)
        recip = 1.0 / jnp.sum(expo, axis=1, keepdims=True)
        probs_low = (expo * recip).astype(jnp.bfloat16)
        output = jnp.dot(probs_low, values, preferred_element_type=jnp.float32)
        delta = jnp.sum(g_head.astype(jnp.float32) * output, axis=1, keepdims=True)
        dprobs = jnp.dot(g_head, values.T, preferred_element_type=jnp.float32)
        dscore = (expo * recip * (dprobs - delta) * scale).astype(jnp.bfloat16)
        pieces.append(
            jnp.dot(dscore, keys, preferred_element_type=jnp.float32).astype(jnp.bfloat16)
        )
        grad_keys = grad_keys + jnp.dot(dscore.T, q_head, preferred_element_type=jnp.float32)
        grad_values = grad_values + jnp.dot(probs_low.T, g_head, preferred_element_type=jnp.float32)
    return (jnp.concatenate(pieces, axis=1), jnp.concatenate([grad_keys, grad_values], axis=1))


def group_positions(stretch_order, block_index, offset, half):
    slots = jnp.arange(stretch_order.shape[0], dtype=jnp.int32)
    wanted = 2 * block_index + offset // half
    picked = jnp.sum(
        jnp.where(slots[None, :] == wanted[:, None], stretch_order[None, :], 0), axis=1
    )
    return picked * half + offset % half


def on_device(query, key, value, grad_out, stretch_order):
    tokens = query.shape[0]
    half = tokens // 2
    width = key.shape[1]
    members = lax.axis_size("inner")
    place = lax.axis_index("inner")
    outer_place = lax.axis_index("outer")
    span = tokens * members
    local_rows = jnp.arange(tokens, dtype=jnp.int32)
    group_rows = jnp.arange(span, dtype=jnp.int32)
    qpos = group_positions(stretch_order, jnp.full((tokens,), place, jnp.int32), local_rows, half)
    kpos = group_positions(stretch_order, group_rows // tokens, group_rows % tokens, half)
    earlier = jnp.broadcast_to(outer_place > 0, (tokens, span))
    allowed = jnp.concatenate([earlier, kpos[None, :] <= qpos[:, None]], axis=1)
    joined = jnp.concatenate([key, value], axis=1)
    own_group = lax.all_gather(joined, "inner", axis=0, tiled=True)
    prior_group = shifted(own_group, "outer", 1)
    both = jnp.concatenate([prior_group, own_group], axis=0)
    dq, dkv = attend_block(query, grad_out, both[:, :width], both[:, width:], allowed)
    returned = shifted(dkv[:span].astype(jnp.bfloat16), "outer", -1).astype(jnp.float32)
    total = lax.psum_scatter(dkv[span:] + returned, "inner", scatter_dimension=0, tiled=True)
    return (dq, total[:, :width].astype(jnp.bfloat16), total[:, width:].astype(jnp.bfloat16))


def solution(mesh):
    return jax.shard_map(
        on_device,
        mesh=mesh,
        in_specs=(
            P(("outer", "inner"), None),
            P(("outer", "inner"), None),
            P(("outer", "inner"), None),
            P(("outer", "inner"), None),
            P(),
        ),
        out_specs=(
            P(("outer", "inner"), None),
            P(("outer", "inner"), None),
            P(("outer", "inner"), None),
        ),
        check_vma=False,
    )
```

profile of v0, /device:TPU:2, one launch (start us, length us, event | category | flops | bytes accessed | tf_op | source)
XLA Modules:
  0.0 406.8 jit_solution(10608132806501116956)
XLA Ops:
  7.2 0.0 all-gather.2.cloned.1.call-start
  7.2 1.4 pad_maximum_fusion.2
  8.6 0.0 all-gather.2.cloned.1.call-update
  8.6 0.0 reduce-scatter.2.cloned.1.call-start
  8.7 83.5 %all-gather.2.cloned.1.call-done = bf16[4096,256]{1,0:T(8,128)(2,1)} async-done(((bf16[128,256]{1,0:T(8,128)(2,1)}), bf16[4096,256]{1,0:T(8,128)(2,1)}) %all-gather.2.cloned.1.call-update) | async-done | bytes 2097168 | tf_op jit(solution)/shard_map/all_gather | solution.py:66
  92.2 2.0 collective-permute-start
  94.2 0.8 fusion.86
  95.0 0.1 copy.22
  95.2 0.1 copy.23
  95.3 0.1 copy.24
  95.4 0.1 copy.25
  95.6 0.7 select_reduce_fusion.1
  96.3 0.9 select_reduce_fusion
  97.3 0.7 broadcast_compare_fusion
  98.0 0.0 copy-start.10
  98.0 22.0 %collective-permute-done = bf16[4096,256]{1,0:T(8,128)(2,1)} collective-permute-done((bf16[4096,256]{1,0:T(8,128)(2,1)}, bf16[4096,256]{1,0:T(8,128)(2,1)}, u32[]{:S(2)}, u32[]{:S(2)}) %collective-permute-start) | collective-permute-done | bytes 2097184 | tf_op jit(solution)/shard_map/ppermute | solution.py:10
  120.0 1.7 constant_dynamic-update-slice_fusion.1
  121.7 0.1 constant_dynamic-update-slice_fusion
  121.9 1.3 fusion.91
  123.1 1.3 fusion.90
  124.4 1.3 fusion.89
  125.6 1.3 fusion.88
  126.9 1.1 fusion.27
  128.0 0.0 copy-done.9
  128.0 0.8 fusion.51
  128.8 1.1 fusion.28
  129.9 1.1 fusion.29
  131.1 1.1 fusion.30
  132.2 1.3 fusion.31
  133.4 1.4 fusion.23
  134.9 0.7 fusion.62
  135.6 1.0 convolution_add_fusion.2
  136.7 1.3 fusion.32
  137.9 1.2 fusion.22
  139.2 0.0 copy-start
  139.2 1.0 convolution_add_fusion.1
  140.2 1.3 fusion.33
  141.5 1.2 fusion.21
  142.8 0.0 copy-start.2
  142.8 1.0 convolution_add_fusion
  143.8 1.3 fusion.34
  145.1 1.2 fusion.20
  146.3 0.0 copy-done
  146.3 0.0 copy-start.4
  146.3 1.0 convolution_add_fusion.5
  147.3 0.7 convolution_add_fusion.4
  148.1 0.0 copy-done.4
  148.1 0.7 convolution_add_fusion.3
  148.8 0.3 fusion.26
  149.1 1.9 collective-permute-start.1
  151.1 23.5 %collective-permute-done.1 = bf16[4096,256]{0,1:T(8,128)(2,1)S(1)} collective-permute-done((bf16[4096,256]{0,1:T(8,128)(2,1)S(1)}, bf16[4096,256]{0,1:T(8,128)(2,1)S(1)}, u32[]{:S(2)}, u32[]{:S(2)}) %collective-permute-start.1) | collective-permute-done | bytes 2097184 | tf_op jit(solution)/shard_map/ppermute | solution.py:10
  174.6 2.5 fusion.25
  177.0 0.0 reduce-scatter.2.cloned.1.call-update
  177.1 0.0 copy-start.1
  177.1 0.0 copy-start.3
  177.1 2.5 convolution_convert_fusion.3
  179.6 2.9 convolution_convert_fusion.2
  182.6 0.8 convolution_convert_fusion.1
  183.4 0.8 convolution_convert_fusion
  184.2 0.8 copy.19
  185.0 212.6 %reduce-scatter.2.cloned.1.call-done = f32[128,256]{0,1:T(8,128)} async-done(((f32[4096,256]{0,1:T(8,128)}), f32[128,256]{0,1:T(8,128)}) %reduce-scatter.2.cloned.1.call-update) | async-done | bytes 131088 | tf_op jit(solution)/shard_map/reduce_scatter | solution.py:71
  397.5 0.9 convert.8
  398.5 0.7 copy.20
  399.2 0.7 copy.21
  (23 shorter events, 0.1 us)
Async XLA Ops:
  7.2 85.0 %all-gather.2.cloned.1.call-start = ((), (), s32[]{:S(2)}) async-start(), calls=%async_computation.1 | async-start | bytes 2162688 | tf_op jit(solution)/shard_map/all_gather | solution.py:66
  8.6 388.9 %reduce-scatter.2.cloned.1.call-start = ((), (), s32[]{:S(2)}) async-start(), calls=%async_computation.2 | async-start | bytes 4325376 | tf_op jit(solution)/shard_map/reduce_scatter | solution.py:71
  92.2 29.5 %copy-start.6 = (bf16[4096,256]{1,0:T(8,128)(2,1)S(1)}, bf16[4096,256]{1,0:T(8,128)(2,1)}, u32[]{:S(2)}) copy-start(bf16[4096,256]{1,0:T(8,128)(2,1)} %all-gather.2.cloned.1.call-done) | copy-start | bytes 6291460
  92.2 27.8 %collective-permute-start = (bf16[4096,256]{1,0:T(8,128)(2,1)}, bf16[4096,256]{1,0:T(8,128)(2,1)}, u32[]{:S(2)}, u32[]{:S(2)}) collective-permute-start(bf16[4096,256]{1,0:T(8,128)(2,1)} %all-gather.2.cloned.1.call-done), channel_id=1, source_target_pairs={{0,32},{32,64},{64,96},{96,128},{128,160},{160,192},{192,224},{1,3... | collective-permute-start | bytes 6291464 | tf_op jit(solution)/shard_map/ppermute | solution.py:10
  98.0 23.9 %copy-start.10 = (bf16[128,512]{1,0:T(8,128)(2,1)S(1)}, bf16[128,512]{1,0:T(8,128)(2,1)}, u32[]{:S(2)}) copy-start(bf16[128,512]{1,0:T(8,128)(2,1)} %param.5) | copy-start | bytes 393220
  121.8 23.2 %copy-start.7 = (bf16[8192,256]{1,0:T(8,128)(2,1)}, bf16[8192,256]{1,0:T(8,128)(2,1)S(1)}, u32[]{:S(2)}) copy-start(bf16[8192,256]{1,0:T(8,128)(2,1)S(1)} %constant_dynamic-update-slice_fusion) | copy-start | bytes 12582916
  126.9 1.1 copy-start.9
  139.2 7.1 %copy-start = (bf16[128,8192]{0,1:T(8,128)(2,1)}, bf16[128,8192]{0,1:T(8,128)(2,1)S(1)}, u32[]{:S(2)}) copy-start(bf16[128,8192]{0,1:T(8,128)(2,1)S(1)} %fusion.22) | copy-start | bytes 6291460
  142.8 4.6 %copy-start.2 = (bf16[128,8192]{0,1:T(8,128)(2,1)}, bf16[128,8192]{0,1:T(8,128)(2,1)S(1)}, u32[]{:S(2)}) copy-start(bf16[128,8192]{0,1:T(8,128)(2,1)S(1)} %fusion.21) | copy-start | bytes 6291460
  146.3 1.8 copy-start.4
  149.1 25.5 %collective-permute-start.1 = (bf16[4096,256]{0,1:T(8,128)(2,1)S(1)}, bf16[4096,256]{0,1:T(8,128)(2,1)S(1)}, u32[]{:S(2)}, u32[]{:S(2)}) collective-permute-start(bf16[4096,256]{0,1:T(8,128)(2,1)S(1)} %fusion.26), channel_id=1, source_target_pairs={{32,0},{64,32},{96,64},{128,96},{160,128},{192,160},{224,192},{33,... | collective-permute-start | bytes 6291464 | tf_op jit(solution)/shard_map/ppermute | solution.py:10
  177.1 2.5 copy-start.1
  177.1 5.5 %copy-start.3 = (bf16[128,8192]{0,1:T(8,128)(2,1)S(1)}, bf16[128,8192]{0,1:T(8,128)(2,1)}, u32[]{:S(2)}) copy-start(bf16[128,8192]{0,1:T(8,128)(2,1)} %copy-done.2) | copy-start | bytes 6291460
  177.1 5.5 %copy-start.8 = (bf16[8192,256]{1,0:T(8,128)(2,1)S(1)}, bf16[8192,256]{1,0:T(8,128)(2,1)}, u32[]{:S(2)}) copy-start(bf16[8192,256]{1,0:T(8,128)(2,1)} %copy-done.7) | copy-start | bytes 12582916
  179.6 3.7 copy-start.5
Sparse Core Ops, SparseCore 0:
  11.2 80.9 all-gather.1
  177.2 220.3 reduce-scatter.1
where the time goes:
time: 407 us
  waiting for transfers between devices  342 us (84%)
  matrix products  29.4 us (7%)
  between operations  14.4 us (4%)
  other arithmetic  11.9 us (3%)
  local copies, waits for them, and re-layouts  5.43 us (1%)
    reduce_scatter x1, waiting for transfers between devices, on_device(): lax.psum_scatter(dkv[span:] + returned, 'inner', scatter_dimension=0, til...  213 us
    all_gather x1, waiting for transfers between devices, on_device(): own_group = lax.all_gather(joined, 'inner', axis=0, tiled=True)  83.5 us
    ppermute x2, waiting for transfers between devices, shifted(): lax.ppermute(value, axis, [(source, source + steps) for source in range(f...  45.5 us
  transfers between devices with their start and end apart: 4, of which 4 were waited for; matrix products, arithmetic and copies ran while one was open for 3% of the time, Pallas kernels for 0%

commit v1 on v0

v1 whole, which is shorter than its diff:
```python
import functools
import jax
import jax.numpy as jnp
from jax import lax
from jax.experimental import pallas as pl
from jax.experimental.pallas import tpu as pltpu
from jax.sharding import PartitionSpec as P

MESH = pl.DeviceIdType.MESH
BF16, F32 = jnp.bfloat16, jnp.float32
NEG = -1e30
T = 128
NY = 4
CH = 256
COMM = True


def kernel(groups, members, q_in, k_in, v_in, g_in, order, dq_out, dk_out, dv_out,
           ka, mk, va, qa, ga, kt, qx, gt, e_buf, d_buf, factor, delta, dvacc, dkacc, dqt,
           stats, dels, dvb, dkb, dqb, pdv, pdk, rdv, rdk, rdq,
           loc, s_k, r_k, s_v, r_v, s_kf, s_vf, s_q, r_q, s_g, r_g, s_st, r_st, s_de, r_de,
           s_p, r_p, s_dv, r_dv, s_dk, r_dk, s_dq, r_dq):
    nz = members // NY
    heads = qa.shape[0]
    width = NY * T
    own_rows = nz * T
    keys = 2 * own_rows
    nch = keys // CH
    scale = float(T) ** -0.5
    cexp = scale * 1.4426950408889634
    outer = lax.axis_index("outer")
    inner = lax.axis_index("inner")
    z, y = inner // NY, inner % NY

    def ypeer(d):
        return (outer, z * NY + (y + d) % NY)

    def zpeer(d):
        return (outer, ((z + d) % nz) * NY + y)

    after = ((outer + 1) % groups, inner)
    before = ((outer + groups - 1) % groups, inner)

    def rcopy(src, dst, ssem, rsem, dev):
        return pltpu.make_async_remote_copy(src_ref=src, dst_ref=dst, send_sem=ssem, recv_sem=rsem,
                                            device_id=dev, device_id_type=MESH)

    far = sorted(range(1, nz), key=lambda d: -min(d, nz - d))
    near = far[::-1]

    def slot(ref, d):
        return ref.at[pl.ds(d * T, T)]

    def head_cols(ref, h):
        return ref.at[:, pl.ds(h * T, T)]

    def k_push(d):
        return rcopy(k_in, slot(ka, nz - d), s_k.at[d], r_k.at[nz - d], zpeer(d))

    def v_push(d):
        return rcopy(v_in, slot(va, nz - d), s_v.at[d], r_v.at[nz - d], zpeer(d))

    def k_forward(d):
        return rcopy(slot(ka, d) if d else k_in, slot(ka, nz + d), s_kf.at[d], r_k.at[nz + d], after)

    def v_forward(d):
        return rcopy(slot(va, d) if d else v_in, slot(va, nz + d), s_vf.at[d], r_v.at[nz + d], after)

    def q_push(h, d):
        return rcopy(q_in.at[:, pl.ds(h * T, T)], qa.at[h, pl.ds((NY - d) * T, T)], s_q.at[h, d], r_q.at[h, NY - d], ypeer(d))

    def g_push(h, d):
        return rcopy(g_in.at[:, pl.ds(h * T, T)], ga.at[h, pl.ds((NY - d) * T, T)], s_g.at[h, d], r_g.at[h, NY - d], ypeer(d))

    def stats_push(h, d):
        return rcopy(stats.at[h, 0], stats.at[h, NY - d], s_st.at[h, d], r_st.at[h, NY - d], ypeer(d))

    def delta_push(h, d):
        return rcopy(dels.at[h, 0], dels.at[h, NY - d], s_de.at[h, d], r_de.at[h, NY - d], ypeer(d))

    def dq_push(h, d):
        return rcopy(dqb.at[h, d], rdq.at[h, NY - d], s_dq.at[h, d], r_dq.at[h, NY - d], ypeer(d))

    def dv_back():
        return rcopy(dvb.at[pl.ds(own_rows, own_rows)], pdv, s_p.at[0], r_p.at[0], before)

    def dk_back():
        return rcopy(dkb.at[pl.ds(own_rows, own_rows)], pdk, s_p.at[1], r_p.at[1], before)

    def dv_push(d):
        return rcopy(slot(dvb, d), rdv.at[nz - d], s_dv.at[d], r_dv.at[nz - d], zpeer(d))

    def dk_push(d):
        return rcopy(slot(dkb, d), rdk.at[nz - d], s_dk.at[d], r_dk.at[nz - d], zpeer(d))

    if COMM:
        peers = [ypeer(d) for d in range(1, NY)] + [zpeer(d) for d in range(1, nz)] + [after, before]
        barrier = pltpu.get_barrier_semaphore()
        for peer in peers:
            pl.semaphore_signal(barrier, inc=1, device_id=peer, device_id_type=MESH)
        pl.semaphore_wait(barrier, len(peers))
        k_forward(0).start()
        for d in far:
            k_push(d).start()
        for h in range(heads):
            for d in (2, 1, 3):
                q_push(h, d).start()
        v_forward(0).start()
        for d in far:
            v_push(d).start()
        for h in range(heads):
            for d in (2, 1, 3):
                g_push(h, d).start()
    locals_ = [
        pltpu.make_async_copy(k_in, slot(ka, 0), loc.at[0]),
        pltpu.make_async_copy(v_in, slot(va, 0), loc.at[1]),
    ]
    for h in range(heads):
        locals_.append(pltpu.make_async_copy(head_cols(q_in, h), qa.at[h, pl.ds(0, T)], loc.at[2 + 2 * h]))
        locals_.append(pltpu.make_async_copy(head_cols(g_in, h), ga.at[h, pl.ds(0, T)], loc.at[3 + 2 * h]))
    for c in locals_:
        c.start()

    nst = 2 * NY
    lane = lax.broadcasted_iota(jnp.int32, (1, T), 1)
    qorder = jnp.full((1, T), 1 << 20, jnp.int32)
    for s in range(nst):
        block = z * NY + (y + s // 2) % NY
        qorder = jnp.where(lane == s, order[2 * block + s % 2], qorder)
    for a in range(2 * nz):
        block = ((z + a // 2) % nz) * NY + y
        row = jnp.where(order[2 * block + a % 2] > qorder, NEG, 0.0)
        mk[pl.ds(a * (T // 2), T // 2), :] = jnp.broadcast_to(row, (T // 2, T)).astype(BF16)
    first = jnp.where(jnp.logical_and(outer == 0, lane < nst), NEG, 0.0)
    mk[pl.ds(own_rows, own_rows), :] = jnp.broadcast_to(first, (own_rows, T)).astype(BF16)
    sub = lax.broadcasted_iota(jnp.int32, (T, width), 0)
    col = lax.broadcasted_iota(jnp.int32, (T, width), 1)
    qx[pl.ds(T, T), :] = jnp.where(sub == col // (T // 2), 1.0, 0.0).astype(BF16)
    o0, o1 = order[2 * inner], order[2 * inner + 1]
    kt_i = lax.broadcasted_iota(jnp.int32, (T, T), 0)
    qt_i = lax.broadcasted_iota(jnp.int32, (T, T), 1)
    half = T // 2
    kpos = jnp.where(kt_i < half, o0, o1) * half + kt_i % half
    qpos = jnp.where(qt_i < half, o0, o1) * half + qt_i % half
    diag = kpos <= qpos

    for c in locals_:
        c.wait()
    if COMM:
        for d in near:
            k_push(nz - d).wait_recv()
            k_forward(d).start()
        for d in [0] + near:
            k_forward(d).wait_recv()

    def rows_of(i):
        return pl.ds(pl.multiple_of(i * CH, CH), CH)

    def stage1(h, carry):
        if COMM:
            for d in range(1, NY):
                q_push(h, d).wait_recv()
        qx[pl.ds(0, T), :] = qa[h].T

        def scores(i):
            rows = rows_of(i)
            left = jnp.concatenate([ka[rows, :], mk[rows, :]], axis=1)
            s = jnp.dot(left, qx[...], preferred_element_type=F32)
            e_buf[h, rows, :] = s
            return s

        def fold(s):
            return s.reshape(CH // 8, 8, width)

        scores(0)
        e_buf[h, pl.ds(0, T), pl.ds(0, T)] = jnp.where(diag, e_buf[h, pl.ds(0, T), pl.ds(0, T)], NEG)
        top8 = jnp.max(fold(e_buf[h, pl.ds(0, CH), :]), axis=0)
        top8 = lax.fori_loop(1, nch, lambda i, t: jnp.maximum(t, jnp.max(fold(scores(i)), axis=0)), top8)
        top = jnp.max(top8, axis=0, keepdims=True)

        def expo(i, acc):
            rows = rows_of(i)
            e = jnp.exp2((e_buf[h, rows, :] - top) * cexp)
            e_buf[h, rows, :] = e
            return acc + jnp.sum(fold(e), axis=0)

        sum8 = lax.fori_loop(0, nch, expo, jnp.zeros((8, width), F32))
        stats[h, 0, pl.ds(0, 1), :] = top
        stats[h, 0, pl.ds(1, 1), :] = jnp.sum(sum8, axis=0, keepdims=True)
        if COMM:
            for d in (2, 1, 3):
                stats_push(h, d).start()
        return carry

    lax.fori_loop(0, heads, stage1, 0)

    def aligned(ref, h, r, row):
        part = ref[h, r, pl.ds(row, 1), :]
        if r == 0:
            return part
        cut = (NY - r) * T
        return jnp.concatenate([part[:, cut:], part[:, :cut]], axis=1)

    if COMM:
        for d in near:
            v_push(nz - d).wait_recv()
            v_forward(d).start()
        for d in [0] + near:
            v_forward(d).wait_recv()
    for i in range(nch):
        kt[i] = ka[pl.ds(i * CH, CH), :].T

    def stage2(h, carry):
        if COMM:
            for d in range(1, NY):
                stats_push(h, d).wait_recv()
                g_push(h, d).wait_recv()
        tops = [aligned(stats, h, r, 0) for r in range(NY)]
        sums = [aligned(stats, h, r, 1) for r in range(NY)]
        top = functools.reduce(jnp.maximum, tops)
        weights = [jnp.exp2((t - top) * cexp) for t in tops]
        total = sum(w * s for w, s in zip(weights, sums))
        f = weights[0] * (1.0 / total)
        factor[h] = f * scale
        gt[...] = ga[h].T

        def body(i, acc):
            rows = rows_of(i)
            pb = (e_buf[h, rows, :] * f).astype(BF16)
            dp = jnp.dot(va[rows, :], gt[...], preferred_element_type=F32)
            d_buf[h, rows, :] = dp
            dvacc[rows, :] = dvacc[rows, :] + jnp.dot(pb, ga[h], preferred_element_type=F32)
            return acc + jnp.sum((pb.astype(F32) * dp).reshape(CH // 8, 8, width), axis=0)

        acc = lax.fori_loop(0, nch, body, jnp.zeros((8, width), F32))
        dels[h, 0] = jnp.sum(acc, axis=0, keepdims=True)
        if COMM:
            for d in (2, 1, 3):
                delta_push(h, d).start()
        return carry

    dvacc[...] = jnp.zeros_like(dvacc)
    dkacc[...] = jnp.zeros_like(dkacc)
    dqt[...] = jnp.zeros_like(dqt)
    lax.fori_loop(0, heads, stage2, 0)
    dvb[pl.ds(own_rows, own_rows), :] = dvacc[pl.ds(own_rows, own_rows), :].astype(BF16)
    if COMM:
        dv_back().start()

    def stage3(lo, hi, first_part, last_part):
        def run(h, carry):
            if first_part:
                if COMM:
                    for d in range(1, NY):
                        delta_push(h, d).wait_recv()
                delta[h] = sum(aligned(dels, h, r, 0) for r in range(NY))
            f, dl = factor[h], delta[h]

            def body(i, c):
                rows = rows_of(i)
                ds = ((e_buf[h, rows, :] * f) * (d_buf[h, rows, :] - dl)).astype(BF16)
                dkacc[rows, :] = dkacc[rows, :] + jnp.dot(ds, qa[h], preferred_element_type=F32)
                dqt[h] = dqt[h] + jnp.dot(kt[i], ds, preferred_element_type=F32)
                return c

            lax.fori_loop(lo // CH, hi // CH, body, 0)
            if last_part:
                for d in range(1, NY):
                    dqb[h, d] = dqt[h, :, pl.ds(d * T, T)].T.astype(BF16)
                if COMM:
                    for d in (2, 1, 3):
                        dq_push(h, d).start()
            return carry

        lax.fori_loop(0, heads, run, 0)

    mid = own_rows // 2
    stage3(own_rows, keys, True, False)
    dkb[pl.ds(own_rows, own_rows), :] = dkacc[pl.ds(own_rows, own_rows), :].astype(BF16)
    if COMM:
        dk_back().start()
        dv_back().wait_recv()
    dvacc[pl.ds(0, own_rows), :] = dvacc[pl.ds(0, own_rows), :] + pdv[...].astype(F32)
    dvb[pl.ds(0, own_rows), :] = dvacc[pl.ds(0, own_rows), :].astype(BF16)
    if COMM:
        for d in far:
            dv_push(d).start()
    stage3(mid, own_rows, False, False)
    if COMM:
        dk_back().wait_recv()
    dkb[pl.ds(mid, mid), :] = (dkacc[pl.ds(mid, mid), :] + pdk[pl.ds(mid, mid), :].astype(F32)).astype(BF16)
    if COMM:
        for d in far:
            if d * T >= mid:
                dk_push(d).start()
    stage3(0, mid, False, True)
    dkacc[pl.ds(0, mid), :] = dkacc[pl.ds(0, mid), :] + pdk[pl.ds(0, mid), :].astype(F32)
    dkb[pl.ds(0, mid), :] = dkacc[pl.ds(0, mid), :].astype(BF16)
    if COMM:
        for d in far:
            if d * T < mid:
                dk_push(d).start()

    if COMM:
        for d in far:
            dv_push(d).wait_recv()
    dv_out[...] = (dvacc[pl.ds(0, T), :] + sum(rdv[nz - d].astype(F32) for d in range(1, nz))).astype(BF16)
    for h in range(heads):
        if COMM:
            for d in range(1, NY):
                dq_push(h, d).wait_recv()
        mine = dqt[h, :, pl.ds(0, T)].T
        dq_out[:, pl.ds(h * T, T)] = (mine + sum(rdq[h, d].astype(F32) for d in range(1, NY))).astype(BF16)
    if COMM:
        for d in far:
            dk_push(d).wait_recv()
    dk_out[...] = (dkacc[pl.ds(0, T), :] + sum(rdk[nz - d].astype(F32) for d in range(1, nz))).astype(BF16)

    if COMM:
        dv_back().wait_send()
        dk_back().wait_send()
        for d in range(nz):
            k_forward(d).wait_send()
            v_forward(d).wait_send()
            if d:
                k_push(d).wait_send()
                v_push(d).wait_send()
                dv_push(d).wait_send()
                dk_push(d).wait_send()
        for h in range(heads):
            for d in range(1, NY):
                for push in (q_push, g_push, stats_push, delta_push, dq_push):
                    push(h, d).wait_send()


def fused(groups, members, query, key, value, grad_out, stretch_order):
    tokens, dh = key.shape
    heads = query.shape[1] // dh
    nz = members // NY
    own = nz * tokens
    keys, width = 2 * own, NY * tokens
    dma = pltpu.SemaphoreType.DMA
    any_spec = pl.BlockSpec(memory_space=pl.ANY)
    vm = pl.BlockSpec(memory_space=pltpu.VMEM)
    V = pltpu.VMEM
    return pl.pallas_call(
        functools.partial(kernel, groups, members),
        out_shape=(jax.ShapeDtypeStruct(query.shape, BF16), jax.ShapeDtypeStruct(key.shape, BF16),
                   jax.ShapeDtypeStruct(value.shape, BF16)),
        in_specs=[any_spec] * 4 + [pl.BlockSpec(memory_space=pltpu.SMEM)],
        out_specs=(vm, vm, vm),
        scratch_shapes=[
            V((keys, dh), BF16), V((keys, dh), BF16), V((keys, dh), BF16),
            V((heads, width, dh), BF16), V((heads, width, dh), BF16),
            V((keys // CH, dh, CH), BF16), V((2 * dh, width), BF16), V((dh, width), BF16),
            V((heads, keys, width), F32), V((heads, keys, width), F32),
            V((heads, 1, width), F32), V((heads, 1, width), F32),
            V((keys, dh), F32), V((keys, dh), F32), V((heads, dh, width), F32),
            V((heads, NY, 2, width), F32), V((heads, NY, 1, width), F32),
            V((keys, dh), BF16), V((keys, dh), BF16), V((heads, NY, tokens, dh), BF16),
            V((own, dh), BF16), V((own, dh), BF16),
            V((nz, tokens, dh), BF16), V((nz, tokens, dh), BF16), V((heads, NY, tokens, dh), BF16),
            dma((2 + 2 * heads,)),
            dma((nz,)), dma((2 * nz,)), dma((nz,)), dma((2 * nz,)), dma((nz,)), dma((nz,)),
            dma((heads, NY)), dma((heads, NY)), dma((heads, NY)), dma((heads, NY)),
            dma((heads, NY)), dma((heads, NY)), dma((heads, NY)), dma((heads, NY)),
            dma((2,)), dma((2,)), dma((nz,)), dma((nz,)), dma((nz,)), dma((nz,)),
            dma((heads, NY)), dma((heads, NY)),
        ],
        name="attention_backward",
        compiler_params=pltpu.CompilerParams(
            **(dict(collective_id=0, has_side_effects=True) if COMM else {}), vmem_limit_bytes=60 << 20),
    )(query, key, value, grad_out, stretch_order)


def solution(mesh):
    groups, members = mesh.shape["outer"], mesh.shape["inner"]
    spec = P(("outer", "inner"), None)
    return jax.shard_map(
        functools.partial(fused, groups, members), mesh=mesh,
        in_specs=(spec, spec, spec, spec, P()), out_specs=(spec, spec, spec), check_vma=False)
```

time: 407 us -> 71.9 us (0.18)
  the two profiles are of different devices: /device:TPU:2 before, /device:TPU:1 now
where the time goes in v1:
time: 71.9 us; the launch traced here: 71.7 us
  Pallas kernels  68.1 us (95%)
  local copies, waits for them, and re-layouts  2.96 us (4%)
    pallas_call x1, Pallas kernels, fused(): pl.pallas_call(functools.partial(kernel, groups, members), out_shape=(jax...  68.1 us
    unnamed x7, local copies, waits for them, and re-layouts  2.96 us

profile of v1, /device:TPU:1, one launch (start us, length us, event | category | flops | bytes accessed | tf_op | source)
XLA Modules:
  0.0 71.7 jit_solution(11195036365569878337)
XLA Ops:
  0.6 68.1 %attention_backward.1 = (bf16[128,512]{1,0:T(8,128)(2,1)}, bf16[128,128]{1,0:T(8,128)(2,1)}, bf16[128,128]{1,0:T(8,128)(2,1)}) custom-call(bf16[128,512]{1,0:T(8,128)(2,1)} %q_in.1, bf16[128,128]{1,0:T(8,128)(2,1)} %k_in.1, bf16[128,128]{1,0:T(8,128)(2,1)} %v_in.1, bf16[128,512]{1,0:T(8,128)(2,1)} %g_in.1, s32[64]{0:T(128)} %order.1), custom_call_target="tpu_custom_call" | custom-call | tf_op jit(solution)/shard_map/attention_backward/pallas_call | solution.py:346
  68.7 0.0 copy-start.1
  68.7 1.6 %copy.11 = bf16[128,512]{1,0:T(8,128)(2,1)} copy(bf16[128,512]{1,0:T(8,128)(2,1)} %get-tuple-element.6) | data formatting | bytes 262144
  70.3 0.0 copy-done.1
  70.3 0.0 copy-start
  70.3 0.6 copy.12
  70.9 0.2 copy-done
  71.1 0.6 copy.13
Async XLA Ops:
  68.7 1.6 %copy-start.1 = (bf16[128,128]{1,0:T(8,128)(2,1)S(1)}, bf16[128,128]{1,0:T(8,128)(2,1)}, u32[]{:S(2)}) copy-start(bf16[128,128]{1,0:T(8,128)(2,1)} %get-tuple-element.7) | copy-start | bytes 98308
  70.3 0.8 %copy-start = (bf16[128,128]{1,0:T(8,128)(2,1)S(1)}, bf16[128,128]{1,0:T(8,128)(2,1)}, u32[]{:S(2)}) copy-start(bf16[128,128]{1,0:T(8,128)(2,1)} %get-tuple-element.8) | copy-start | bytes 98308

commit v2 on v0

v2 whole, which is shorter than its diff:
```python
import functools
import jax
import jax.numpy as jnp
from jax import lax
from jax.experimental import pallas as pl
from jax.experimental.pallas import tpu as pltpu
from jax.sharding import PartitionSpec as P

MESH = pl.DeviceIdType.MESH
BF16, F32 = jnp.bfloat16, jnp.float32
NEG = -1e30
T = 128
NY = 4
CS = 256
CC = 1024
CD = 512
COMM = True
TN = 0
BARZ = (1, 2, 6, 7)
BARY = (1, 3)


def kernel(groups, members, q_in, k_in, v_in, g_in, order, dq_out, dk_out, dv_out,
           ka, mk, va, qa, ga, kt, qx, gx, e_buf, d_buf, dvacc, dkacc, dqt,
           stats, dels, tops8, sums8, dvb, dkb, dvp, dkp, dqb, pdv, pdk, rdv, rdk, rdvp, rdkp, rdq,
           loc, s_k, r_k, s_v, r_v, s_kf, s_vf, s_q, r_q, s_g, r_g, s_st, r_st, s_de, r_de,
           s_p, r_p, s_dv, r_dv, s_dk, r_dk, s_dvp, r_dvp, s_dkp, r_dkp, s_dq, r_dq):
    nz = members // NY
    heads = qa.shape[0]
    width = NY * T
    own_rows = nz * T
    keys = 2 * own_rows
    scale = float(T) ** -0.5
    cexp = scale * 1.4426950408889634
    outer = lax.axis_index("outer")
    inner = lax.axis_index("inner")
    z, y = inner // NY, inner % NY
    after = ((outer + 1) % groups, inner)
    before = ((outer + groups - 1) % groups, inner)
    near = sorted(range(1, nz), key=lambda d: (min(d, nz - d), d))
    far = near[::-1]
    place = {d: i for i, d in enumerate([0] + near)}
    ydist = (2, 1, 3)
    mid = nz // 2

    def ypeer(d):
        return (outer, z * NY + (y + d) % NY)

    def zpeer(d):
        return (outer, ((z + d) % nz) * NY + y)

    def at(ref, d, prior=False):
        return ref.at[pl.ds(place[d] * T + (own_rows if prior else 0), T)]

    def cols(ref, h):
        return ref.at[:, pl.ds(h * T, T)]

    def copy_of(kind, h, d):
        if kind in ("k", "v"):
            ref, src, ssem, rsem = (ka, k_in, s_k, r_k) if kind == "k" else (va, v_in, s_v, r_v)
            s, e = h
            return (at(ref, s) if s else src, at(ref, d), ssem.at[d], rsem.at[d], zpeer(e))
        if kind in ("kf", "vf"):
            ref, src, ssem, rsem = (ka, k_in, s_kf, r_k) if kind == "kf" else (va, v_in, s_vf, r_v)
            return (at(ref, d) if d else src, at(ref, d, True), ssem.at[d], rsem.at[nz + d], after)
        if kind == "q":
            return (cols(q_in, h), qa.at[h, pl.ds((NY - d) * T, T)], s_q.at[h, d], r_q.at[h, NY - d], ypeer(d))
        if kind == "g":
            return (cols(g_in, h), ga.at[h, pl.ds((NY - d) * T, T)], s_g.at[h, d], r_g.at[h, NY - d], ypeer(d))
        if kind in ("qr", "gr"):
            ref, ssem, rsem = (qa, s_q, r_q) if kind == "qr" else (ga, s_g, r_g)
            return (ref.at[h, pl.ds((NY - d) * T, T)], ref.at[h, pl.ds(2 * T, T)], ssem.at[h, 2], rsem.at[h, 2], ypeer(d))
        if kind == "stats":
            return (stats.at[h, 0], stats.at[h, NY - d], s_st.at[h, d], r_st.at[h, NY - d], ypeer(d))
        if kind == "delta":
            return (dels.at[h, 0], dels.at[h, NY - d], s_de.at[h, d], r_de.at[h, NY - d], ypeer(d))
        if kind == "dq":
            return (dqb.at[h, d], rdq.at[h, NY - d], s_dq.at[h, d], r_dq.at[h, NY - d], ypeer(d))
        if kind in ("pdv", "pdk"):
            src, dst = (dvacc, pdv) if kind == "pdv" else (dkacc, pdk)
            i = d + (2 if kind == "pdk" else 0)
            return (src.at[pl.ds(own_rows + d * mid * T, mid * T)], dst.at[pl.ds(d * mid * T, mid * T)],
                    s_p.at[i], r_p.at[i], before)
        if kind in ("dvp", "dkp"):
            src, dst, ssem, rsem = (dvp, rdvp, s_dvp, r_dvp) if kind == "dvp" else (dkp, rdkp, s_dkp, r_dkp)
            return (at(src, d), dst.at[(nz - d) % nz], ssem.at[d], rsem.at[(nz - d) % nz],
                    (before[0], ((z + d) % nz) * NY + y))
        if kind == "dv":
            return (at(dvb, d), rdv.at[nz - d], s_dv.at[d], r_dv.at[nz - d], zpeer(d))
        return (at(dkb, d), rdk.at[nz - d], s_dk.at[d], r_dk.at[nz - d], zpeer(d))

    started, received = [], set()

    def remote(key):
        src, dst, ssem, rsem, dev = copy_of(*key)
        return pltpu.make_async_remote_copy(src_ref=src, dst_ref=dst, send_sem=ssem, recv_sem=rsem,
                                            device_id=dev, device_id_type=MESH)

    def start(kind, h=0, ds=(0,)):
        for d in ds:
            started.append((kind, h, d))
            if COMM:
                remote((kind, h, d)).start()

    def recv(kind, h=0, ds=(0,)):
        for d in ds:
            if (kind, h, d) in received:
                continue
            received.add((kind, h, d))
            if COMM:
                remote((kind, h, d)).wait_recv()

    def ring_start(kind, s, steps):
        for e in steps:
            start(kind, (s, e % nz), ((s - e) % nz,))

    def ring_recv(kind, ds):
        for d in ds:
            recv(kind, (0, nz - d), (d,))

    def on_core(core, work):
        if COMM:
            pl.when(outer % 2 == core)(work)
        elif core == 1:
            work()

    def finish():
        if COMM:
            for key in started:
                remote(key).wait_send()

    locals_ = [pltpu.make_async_copy(k_in, at(ka, 0), loc.at[0]), pltpu.make_async_copy(v_in, at(va, 0), loc.at[1])]
    for h in range(heads):
        locals_.append(pltpu.make_async_copy(cols(q_in, h), qa.at[h, pl.ds(0, T)], loc.at[2 + 2 * h]))
        locals_.append(pltpu.make_async_copy(cols(g_in, h), ga.at[h, pl.ds(0, T)], loc.at[3 + 2 * h]))
    for c in locals_:
        c.start()
    if COMM:
        peers = [ypeer(d) for d in BARY] + [zpeer(d) for d in BARZ] + [after, before]
        barrier = pltpu.get_barrier_semaphore()
        for peer in peers:
            pl.semaphore_signal(barrier, inc=1, device_id=peer, device_id_type=MESH)
        pl.semaphore_wait(barrier, len(peers))
    two, six = 2, nz - 2
    ring_start("k", 0, (2, -2, 1, -1))
    start("kf")
    for h in range(heads):
        start("q", h, (1, 3))

    def start_vg():
        ring_start("v", 0, (2, -2, 1, -1))
        start("vf")
        for h in range(heads):
            start("g", h, (1, 3))

    nst = 2 * NY
    half = T // 2
    lane = lax.broadcasted_iota(jnp.int32, (1, T), 1)
    qorder = jnp.full((1, T), 1 << 20, jnp.int32)
    for s in range(nst):
        block = z * NY + (y + s // 2) % NY
        qorder = jnp.where(lane == s, order[2 * block + s % 2], qorder)
    for d in range(nz):
        block = ((z + d) % nz) * NY + y
        for i in range(2):
            row = jnp.where(order[2 * block + i] > qorder, NEG, 0.0)
            mk[pl.ds(place[d] * T + i * half, half), :] = jnp.broadcast_to(row, (half, T)).astype(BF16)
    first = jnp.where(jnp.logical_and(outer == 0, lane < nst), NEG, 0.0)
    mk[pl.ds(own_rows, own_rows), :] = jnp.broadcast_to(first, (own_rows, T)).astype(BF16)
    sub = lax.broadcasted_iota(jnp.int32, (T, width), 0)
    col = lax.broadcasted_iota(jnp.int32, (T, width), 1)
    onehot = jnp.where(sub == col // half, 1.0, 0.0).astype(BF16)
    for h in range(heads):
        qx[h, pl.ds(T, T), :] = onehot
    o0, o1 = order[2 * inner], order[2 * inner + 1]
    kt_i = lax.broadcasted_iota(jnp.int32, (T, T), 0)
    qt_i = lax.broadcasted_iota(jnp.int32, (T, T), 1)
    kpos = jnp.where(kt_i < half, o0, o1) * half + kt_i % half
    qpos = jnp.where(qt_i < half, o0, o1) * half + qt_i % half
    dvacc[...] = jnp.zeros_like(dvacc)
    dkacc[...] = jnp.zeros_like(dkacc)
    dqt[...] = jnp.zeros_like(dqt)

    for c in locals_:
        c.wait()

    def fold(x):
        return x.reshape(x.shape[0] // 8, 8, width)

    tops, sums = {}, {}

    def pass_a(h, lo, hi):
        lo, hi = lo * T, hi * T
        if lo == 0:
            recv("qr", h, turn(h))
            qx[h, pl.ds(0, T), :] = qa[h].T
        rows = pl.ds(lo, hi - lo)
        left = jnp.concatenate([ka[rows, :], mk[rows, :]], axis=1)
        s = jnp.dot(left, qx[h], preferred_element_type=F32)
        if lo == 0:
            t = jnp.where(kpos <= qpos, s[:T, :T], NEG)
            s = jnp.concatenate([jnp.concatenate([t, s[:T, T:]], axis=1), s[T:]], axis=0)
        e_buf[h, rows, :] = s
        m = jnp.max(fold(s), axis=0)
        tops8[h] = m if lo == 0 else jnp.maximum(tops8[h], m)

    def exponentials(h):
        top = jnp.max(tops8[h], axis=0, keepdims=True)
        l = jnp.zeros((8, width), F32)
        for i in range(keys // CS):
            rows = pl.ds(i * CS, CS)
            e = jnp.exp2((e_buf[h, rows, :] - top) * cexp)
            e_buf[h, rows, :] = e
            l = l + jnp.sum(fold(e), axis=0)
        stats[h, 0, pl.ds(0, 1), :] = top
        stats[h, 0, pl.ds(1, 1), :] = jnp.sum(l, axis=0, keepdims=True)
        start("stats", h, ydist)

    def prepare(h):
        recv("gr", h, turn(h))
        g = ga[h].T.astype(F32) * scale
        g_hi = g.astype(BF16)
        gx[h, pl.ds(0, T), :] = g_hi
        gx[h, pl.ds(T, T), :] = (g - g_hi.astype(F32)).astype(BF16)

    def dprobs(h, lo):
        rows = pl.ds(lo, own_rows)
        v = va[rows, :]
        d_buf[h, rows, :] = jnp.dot(jnp.concatenate([v, v], axis=1), gx[h], preferred_element_type=F32)

    def turn(h):
        return (3,) if h % 2 == 0 else (1,)

    def each_head(work, h0=0, h1=None):
        h1 = heads if h1 is None else h1
        for h in range(h0, h1):
            work(h)

    def wait_y(kind, h):
        if COMM:
            for d in ydist:
                remote((kind, h, d)).wait_recv()

    def forward(kind, ds):
        ring_recv(kind, ds)
        start(kind + "f", 0, ds)

    def relay(kind):
        for h in range(heads):
            recv(kind, h, (1, 3))
            start(kind + "r", h, turn(h))

    ring_recv("k", (six, two))
    ring_start("k", six, (1,))
    ring_start("k", two, (-1, -2))
    start("kf", 0, (six, two))
    relay("q")
    forward("k", (nz - 1, 1))
    start_vg()
    for h in range(heads):
        pass_a(h, 0, 5)
    forward("k", (3, nz - 3, mid))
    ring_recv("v", (six, two))
    ring_start("v", two, (-1,))
    ring_start("v", six, (1, 2))
    relay("g")
    start("vf", 0, (six, two))
    forward("v", (1, nz - 1))
    for h in range(heads):
        pass_a(h, 5, 8)
    recv("kf", 0, (0, 1, nz - 1, two, six))
    for h in range(heads):
        pass_a(h, 8, 13)
    forward("v", (3, nz - 3, mid))
    recv("kf", 0, (3, nz - 3, mid))
    for h in range(heads):
        pass_a(h, 13, 16)
    for h in range(heads):
        exponentials(h)
    for h in range(heads):
        prepare(h)
    for i in range(keys // CD):
        kt[i] = ka[pl.ds(i * CD, CD), :].T
    for h in range(heads):
        dprobs(h, 0)
    recv("vf", 0, [0] + near)
    for h in range(heads):
        dprobs(h, own_rows)

    def aligned(ref, h, r, row):
        part = ref[h, r, pl.ds(row, 1), :]
        if r == 0:
            return part
        cut = (NY - r) * T
        return jnp.concatenate([part[:, cut:], part[:, :cut]], axis=1)

    def second(h):
        wait_y("stats", h)
        parts = [aligned(stats, h, r, 0) for r in range(NY)]
        top = functools.reduce(jnp.maximum, parts)
        weights = [jnp.exp2((t - top) * cexp) for t in parts]
        total = sum(w * aligned(stats, h, r, 1) for r, w in enumerate(weights))
        f = weights[0] * (1.0 / total)
        acc = jnp.zeros((8, width), F32)
        for i in range(keys // CC):
            rows = pl.ds(i * CC, CC)
            p = e_buf[h, rows, :] * f
            e_buf[h, rows, :] = p
            pb = p.astype(BF16)
            dvacc[rows, :] = dvacc[rows, :] + jnp.dot(pb, ga[h], preferred_element_type=F32)
            acc = acc + jnp.sum(fold(pb.astype(F32) * d_buf[h, rows, :]), axis=0)
        dels[h, 0] = jnp.sum(acc, axis=0, keepdims=True)
        if COMM:
            for d in ydist:
                remote(("delta", h, d)).start()

    each_head(second)
    for h in range(heads):
        started.extend([("delta", h, d) for d in ydist])
    own = pl.ds(0, own_rows)
    prior = pl.ds(own_rows, own_rows)

    def each(kind, ds, act):
        if COMM:
            for d in ds:
                getattr(remote((kind, 0, d)), act)()

    @functools.partial(on_core, 0)
    def _():
        dvp[...] = dvacc[prior, :].astype(BF16)
        each("dvp", [0] + far, "start")

    @functools.partial(on_core, 1)
    def _():
        each("pdv", (0, 1), "start")
        dvb[...] = dvacc[own, :].astype(BF16)
        each("dv", far, "start")

    def dq_part(h, d):
        return dqt[h, pl.ds(d * T, T), :] if TN else dqt[h, :, pl.ds(d * T, T)].T

    def third(h, lo, n, first, last):
        if first:
            wait_y("delta", h)
        delta = sum(aligned(dels, h, r, 0) for r in range(NY))
        dq = None
        for i in range(lo * T // CD, (lo + n) * T // CD):
            rows = pl.ds(i * CD, CD)
            ds = (e_buf[h, rows, :] * (d_buf[h, rows, :] - delta)).astype(BF16)
            dkacc[rows, :] = dkacc[rows, :] + jnp.dot(ds, qa[h], preferred_element_type=F32)
            if TN:
                term = lax.dot_general(ds, ka[rows, :], (((0,), (0,)), ((), ())), preferred_element_type=F32)
            else:
                term = jnp.dot(kt[i], ds, preferred_element_type=F32)
            dq = term if dq is None else dq + term
        dqt[h] = dq if first else dqt[h] + dq
        if last:
            for d in ydist:
                dqb[h, d] = dq_part(h, d).astype(BF16)
            if COMM:
                for d in ydist:
                    remote(("dq", h, d)).start()

    def part_of(i):
        return [d for d in [0] + far if place[d] // mid == i]

    def prior_dk(i):
        rows, mine = pl.ds(own_rows + i * mid * T, mid * T), pl.ds(i * mid * T, mid * T)

        @functools.partial(on_core, 0)
        def _():
            dkp[mine, :] = dkacc[rows, :].astype(BF16)
            each("dkp", part_of(i), "start")

        @functools.partial(on_core, 1)
        def _():
            each("pdk", (i,), "start")

    def own_dk(i):
        mine = pl.ds(i * mid * T, mid * T)

        @functools.partial(on_core, 0)
        def _():
            each("pdk", (i,), "wait_recv")
            dkacc[mine, :] = dkacc[mine, :] + pdk[mine, :]

        dkb[mine, :] = dkacc[mine, :].astype(BF16)
        each("dk", [d for d in part_of(i) if d], "start")

    each_head(lambda h: third(h, nz + mid, mid, True, False))
    prior_dk(1)
    each_head(lambda h: third(h, nz, mid, False, False))
    prior_dk(0)

    @functools.partial(on_core, 0)
    def _():
        each("pdv", (0, 1), "wait_recv")
        dvacc[own, :] = dvacc[own, :] + pdv[...]
        dvb[...] = dvacc[own, :].astype(BF16)
        each("dv", far, "start")

    each_head(lambda h: third(h, mid, mid, False, False))
    own_dk(1)
    each_head(lambda h: third(h, 0, mid, False, True))
    own_dk(0)

    me = pl.ds(0, T)
    each("dv", far, "wait_recv")
    dvacc[me, :] = dvacc[me, :] + sum(rdv[d].astype(F32) for d in range(1, nz))
    for h in range(heads):
        wait_y("dq", h)
        dq_out[:, pl.ds(h * T, T)] = (dq_part(h, 0) + sum(rdq[h, d].astype(F32) for d in range(1, NY))).astype(BF16)
    each("dk", far, "wait_recv")
    dkacc[me, :] = dkacc[me, :] + sum(rdk[d].astype(F32) for d in range(1, nz))

    @functools.partial(on_core, 1)
    def _():
        each("dvp", [0] + far, "wait_recv")
        each("dkp", [0] + far, "wait_recv")
        dvacc[me, :] = dvacc[me, :] + sum(rdvp[d].astype(F32) for d in range(nz))
        dkacc[me, :] = dkacc[me, :] + sum(rdkp[d].astype(F32) for d in range(nz))

    dv_out[...] = dvacc[me, :].astype(BF16)
    dk_out[...] = dkacc[me, :].astype(BF16)
    finish()
    each("dv", far, "wait_send")
    each("dk", far, "wait_send")
    for h in range(heads):
        each_y = [remote(("dq", h, d)) for d in ydist]
        for c in each_y if COMM else []:
            c.wait_send()

    @functools.partial(on_core, 0)
    def _():
        each("dvp", [0] + far, "wait_send")
        each("dkp", [0] + far, "wait_send")

    @functools.partial(on_core, 1)
    def _():
        each("pdv", (0, 1), "wait_send")
        each("pdk", (0, 1), "wait_send")


def fused(groups, members, query, key, value, grad_out, stretch_order):
    tokens, dh = key.shape
    heads = query.shape[1] // dh
    nz = members // NY
    own = nz * tokens
    keys, width = 2 * own, NY * tokens
    dma = pltpu.SemaphoreType.DMA
    any_spec = pl.BlockSpec(memory_space=pl.ANY)
    vm = pl.BlockSpec(memory_space=pltpu.VMEM)
    V = pltpu.VMEM
    results = pl.pallas_call(
        functools.partial(kernel, groups, members),
        out_shape=(jax.ShapeDtypeStruct(query.shape, BF16), jax.ShapeDtypeStruct(key.shape, BF16),
                   jax.ShapeDtypeStruct(value.shape, BF16)),
        in_specs=[any_spec] * 4 + [pl.BlockSpec(memory_space=pltpu.SMEM)],
        out_specs=(vm, vm, vm),
        scratch_shapes=[
            V((keys, dh), BF16), V((keys, dh), BF16), V((keys, dh), BF16),
            V((heads, width, dh), BF16), V((heads, width, dh), BF16),
            V((keys // CD, dh, CD), BF16), V((heads, 2 * dh, width), BF16), V((heads, 2 * dh, width), BF16),
            V((heads, keys, width), F32), V((heads, keys, width), F32),
            V((keys, dh), F32), V((keys, dh), F32),
            V((heads, width, dh) if TN else (heads, dh, width), F32),
            V((heads, NY, 2, width), F32), V((heads, NY, 1, width), F32),
            V((heads, 8, width), F32), V((heads, 8, width), F32),
            V((own, dh), BF16), V((own, dh), BF16), V((own, dh), BF16), V((own, dh), BF16),
            V((heads, NY, tokens, dh), BF16),
            V((own, dh), F32), V((own, dh), F32),
            V((nz, tokens, dh), BF16), V((nz, tokens, dh), BF16), V((nz, tokens, dh), BF16), V((nz, tokens, dh), BF16),
            V((heads, NY, tokens, dh), BF16),
            dma((2 + 2 * heads,)),
            dma((nz,)), dma((2 * nz,)), dma((nz,)), dma((2 * nz,)), dma((nz,)), dma((nz,)),
            dma((heads, NY)), dma((heads, NY)), dma((heads, NY)), dma((heads, NY)),
            dma((heads, NY)), dma((heads, NY)), dma((heads, NY)), dma((heads, NY)),
            dma((4,)), dma((4,)),
            dma((nz,)), dma((nz,)), dma((nz,)), dma((nz,)), dma((nz,)), dma((nz,)), dma((nz,)), dma((nz,)),
            dma((heads, NY)), dma((heads, NY)),
        ],
        name="attention_backward",
        compiler_params=pltpu.CompilerParams(
            **(dict(collective_id=0, has_side_effects=True) if COMM else {}), vmem_limit_bytes=60 << 20),
    )(query, key, value, grad_out, stretch_order)
    return results


def solution(mesh):
    groups, members = mesh.shape["outer"], mesh.shape["inner"]
    spec = P(("outer", "inner"), None)
    return jax.shard_map(
        functools.partial(fused, groups, members), mesh=mesh,
        in_specs=(spec, spec, spec, spec, P()), out_specs=(spec, spec, spec), check_vma=False)
```

time: 407 us -> 56.6 us (0.14)
  waiting for transfers between devices: 342 us -> 0 us
  Pallas kernels: 0 us -> 52.8 us
  matrix products: 29.4 us -> 0 us
  between operations: 14.4 us -> 0.65 us
  other arithmetic: 11.9 us -> 0 us
    reduce_scatter x1 -> x0, waiting for transfers between devices: 213 us -> none  [on_device(): lax.psum_scatter(dkv[span:] + returned, 'inner', scatter_dimension=0, til...]
    all_gather x1 -> x0, waiting for transfers between devices: 83.5 us -> none  [on_device(): own_group = lax.all_gather(joined, 'inner', axis=0, tiled=True)]
    pallas_call x0 -> x1, Pallas kernels: none -> 52.8 us  [fused(): pl.pallas_call(functools.partial(kernel, groups, members), out_shape=(jax...]
    ppermute x2 -> x0, waiting for transfers between devices: 45.5 us -> none  [shifted(): lax.ppermute(value, axis, [(source, source + steps) for source in range(f...]
    dot_general x24 -> x0, matrix products: 29.4 us -> none  [the longest x4 6.99 us: attend_block(): jnp.dot(dscore, keys, preferred_element_type=jnp.float32)]
    reduce_sum x6 -> x0, other arithmetic: 6.06 us -> none  [the longest x4 4.42 us: attend_block(): recip = 1.0 / jnp.sum(expo, axis=1, keepdims=True)]
  transfers between devices with their start and end apart: 4 -> 0, of which waited for: 4 -> 0; matrix products, arithmetic and copies ran while one was open for 3% -> 0% of each run, Pallas kernels for 0% -> 0%
where the time goes in v2:
time: 56.6 us; the launch traced here: 56.5 us
  Pallas kernels  52.8 us (93%)
  local copies, waits for them, and re-layouts  2.96 us (5%)
  between operations  0.65 us (1%)
    pallas_call x1, Pallas kernels, fused(): pl.pallas_call(functools.partial(kernel, groups, members), out_shape=(jax...  52.8 us
    unnamed x7, local copies, waits for them, and re-layouts  2.96 us

profile of v2, /device:TPU:2, one launch (start us, length us, event | category | flops | bytes accessed | tf_op | source)
XLA Modules:
  0.0 56.5 jit_solution(6742102018371901142)
XLA Ops:
  0.6 52.8 %attention_backward.1 = (bf16[128,512]{1,0:T(8,128)(2,1)}, bf16[128,128]{1,0:T(8,128)(2,1)}, bf16[128,128]{1,0:T(8,128)(2,1)}) custom-call(bf16[128,512]{1,0:T(8,128)(2,1)} %q_in.1, bf16[128,128]{1,0:T(8,128)(2,1)} %k_in.1, bf16[128,128]{1,0:T(8,128)(2,1)} %v_in.1, bf16[128,512]{1,0:T(8,128)(2,1)} %g_in.1, s32[64]{0:T(128)} %order.1), custom_call_target="tpu_custom_call" | custom-call | tf_op jit(solution)/shard_map/attention_backward/pallas_call | solution.py:454
  53.5 0.0 copy-start.1
  53.5 1.6 %copy.11 = bf16[128,512]{1,0:T(8,128)(2,1)} copy(bf16[128,512]{1,0:T(8,128)(2,1)} %get-tuple-element.6) | data formatting | bytes 262144
  55.1 0.0 copy-done.1
  55.1 0.0 copy-start
  55.1 0.6 %copy.12 = bf16[128,128]{1,0:T(8,128)(2,1)} copy(bf16[128,128]{1,0:T(8,128)(2,1)S(1)} %copy-done.1) | data formatting | bytes 65536
  55.7 0.2 copy-done
  55.8 0.6 %copy.13 = bf16[128,128]{1,0:T(8,128)(2,1)} copy(bf16[128,128]{1,0:T(8,128)(2,1)S(1)} %copy-done) | data formatting | bytes 65536
Async XLA Ops:
  53.5 1.6 %copy-start.1 = (bf16[128,128]{1,0:T(8,128)(2,1)S(1)}, bf16[128,128]{1,0:T(8,128)(2,1)}, u32[]{:S(2)}) copy-start(bf16[128,128]{1,0:T(8,128)(2,1)} %get-tuple-element.7) | copy-start | bytes 98308
  55.1 0.8 %copy-start = (bf16[128,128]{1,0:T(8,128)(2,1)S(1)}, bf16[128,128]{1,0:T(8,128)(2,1)}, u32[]{:S(2)}) copy-start(bf16[128,128]{1,0:T(8,128)(2,1)} %get-tuple-element.8) | copy-start | bytes 98308

commit v3 on v2

--- a/solution.py
+++ b/solution.py
@@ -17,7 +17,7 @@
 COMM = True
 TN = 0
 BARZ = (1, 2, 6, 7)
-BARY = (1, 3)
+BARY = (1, 2, 3)
 
 
 def kernel(groups, members, q_in, k_in, v_in, g_in, order, dq_out, dk_out, dv_out,
@@ -145,7 +145,7 @@
     ring_start("k", 0, (2, -2, 1, -1))
     start("kf")
     for h in range(heads):
-        start("q", h, (1, 3))
+        start("q", h, ydist)
 
     def start_vg():
         ring_start("v", 0, (2, -2, 1, -1))
@@ -192,7 +192,7 @@
     def pass_a(h, lo, hi):
         lo, hi = lo * T, hi * T
         if lo == 0:
-            recv("qr", h, turn(h))
+            recv("q", h, ydist)
             qx[h, pl.ds(0, T), :] = qa[h].T
         rows = pl.ds(lo, hi - lo)
         left = jnp.concatenate([ka[rows, :], mk[rows, :]], axis=1)
@@ -254,7 +254,6 @@
     ring_start("k", six, (1,))
     ring_start("k", two, (-1, -2))
     start("kf", 0, (six, two))
-    relay("q")
     forward("k", (nz - 1, 1))
     start_vg()
     for h in range(heads):

time: 56.6 us -> 56.2 us (level)
  no operation moved by 1% of the time
where the time goes in v3:
time: 56.2 us; the launch traced here: 56.1 us
  Pallas kernels  52.4 us (93%)
  local copies, waits for them, and re-layouts  2.96 us (5%)
  between operations  0.65 us (1%)
    pallas_call x1, Pallas kernels, fused(): pl.pallas_call(functools.partial(kernel, groups, members), out_shape=(jax...  52.4 us
    unnamed x7, local copies, waits for them, and re-layouts  2.96 us

profile of v3, /device:TPU:2, one launch (start us, length us, event | category | flops | bytes accessed | tf_op | source)
XLA Modules:
  0.0 56.1 jit_solution(9461652947319453955)
XLA Ops:
  0.6 52.4 %attention_backward.1 = (bf16[128,512]{1,0:T(8,128)(2,1)}, bf16[128,128]{1,0:T(8,128)(2,1)}, bf16[128,128]{1,0:T(8,128)(2,1)}) custom-call(bf16[128,512]{1,0:T(8,128)(2,1)} %q_in.1, bf16[128,128]{1,0:T(8,128)(2,1)} %k_in.1, bf16[128,128]{1,0:T(8,128)(2,1)} %v_in.1, bf16[128,512]{1,0:T(8,128)(2,1)} %g_in.1, s32[64]{0:T(128)} %order.1), custom_call_target="tpu_custom_call" | custom-call | tf_op jit(solution)/shard_map/attention_backward/pallas_call | solution.py:453
  53.1 0.0 copy-start.1
  53.1 1.6 %copy.11 = bf16[128,512]{1,0:T(8,128)(2,1)} copy(bf16[128,512]{1,0:T(8,128)(2,1)} %get-tuple-element.6) | data formatting | bytes 262144
  54.7 0.0 copy-done.1
  54.7 0.0 copy-start
  54.7 0.6 %copy.12 = bf16[128,128]{1,0:T(8,128)(2,1)} copy(bf16[128,128]{1,0:T(8,128)(2,1)S(1)} %copy-done.1) | data formatting | bytes 65536
  55.3 0.2 copy-done
  55.4 0.6 %copy.13 = bf16[128,128]{1,0:T(8,128)(2,1)} copy(bf16[128,128]{1,0:T(8,128)(2,1)S(1)} %copy-done) | data formatting | bytes 65536
Async XLA Ops:
  53.1 1.6 %copy-start.1 = (bf16[128,128]{1,0:T(8,128)(2,1)S(1)}, bf16[128,128]{1,0:T(8,128)(2,1)}, u32[]{:S(2)}) copy-start(bf16[128,128]{1,0:T(8,128)(2,1)} %get-tuple-element.7) | copy-start | bytes 98308
  54.7 0.8 %copy-start = (bf16[128,128]{1,0:T(8,128)(2,1)S(1)}, bf16[128,128]{1,0:T(8,128)(2,1)}, u32[]{:S(2)}) copy-start(bf16[128,128]{1,0:T(8,128)(2,1)} %get-tuple-element.8) | copy-start | bytes 98308
